TPU v7x, 32 devices: a whole 2x2x4 slice. The times are simulated.
32 devices in a mesh: parts: 2 (over x), trade: 16 (over z, y, core).
Axes of the slice: x: 2, y: 2, z: 4, core: 2. Of those that a mesh axis runs over, the one named last changes fastest.
Arguments:
- panels: bfloat16 [2, 256, 4096], P(None, 'parts', 'trade'), parts along dimension 1, may hold values from -6 to 6
- lin_weight: bfloat16 [1024, 4, 128, 128], P(('parts', 'trade')), parts along dimension 0, may hold values from -0.25 to 0.25
- quad_weight: bfloat16 [1024, 4, 128, 128], P(('parts', 'trade')), parts along dimension 0, may hold values from -0.25 to 0.25
- positions: float32 [1024, 128], P(('parts', 'trade')), parts along dimension 0, may hold values from -6 to 6
- pattern: int32 [1024, 4], P(('parts', 'trade')), parts along dimension 0, may hold values from 0 to 31, all different within a row
- netting: int32 [1024], P(('parts', 'trade')), parts along dimension 0, may hold values from 0 to 127
- default_curve: float32 [100], replicated, may hold values from 0.5 to 2
- date_ids: int32 [2], replicated, may hold values from 0 to 99
- loss_given: float32 [256], P('parts'), parts along dimension 0, may hold values from 0.3 to 0.9
Outputs:
- charge: float32 [4], P('parts'), parts along dimension 0
- panel_grad: float32 [2, 256, 4096], P(None, 'parts', 'trade'), parts along dimension 1
There are 2 independent parts, one for each index of `parts`. A program takes and returns all parts, laid end to end along the dimension named above; an argument that names none is the same for every part. Nothing has to cross between parts.
Inputs may be any that keep to these rules, and one draw needn't show every extreme that they name: `pattern`: the 4 factor blocks of a trade block are distinct; every factor block is used by some trade block.
All inputs are finite; a program needn't handle non-finite values.
Results may differ from a plain program's by a relative error of at most 0.0029.
Values may be sent and summed in bfloat16 or wider, within the bound.
A program may use at most 128 MiB of HBM per device.

v0:
```python
import jax
import jax.numpy as jnp
from jax import lax
from jax.sharding import PartitionSpec as P

PICKS = 4
NETS = 128


def per_device(
    panels,
    lin_weight,
    quad_weight,
    positions,
    pattern,
    netting,
    default_curve,
    date_ids,
    loss_given,
):
    devices = lax.axis_size("trade")
    local_blocks, block_width = positions.shape
    trades_all = local_blocks * block_width * devices
    norm_scale = (NETS / trades_all) ** 0.5
    grad_unit = 1.0 / norm_scale
    factors = panels.shape[2] * devices
    fblocks = factors // block_width
    horizon = jnp.arange(default_curve.shape[0], dtype=jnp.int32)
    weights = jnp.sum(
        jnp.where(date_ids[:, None] == horizon[None, :], default_curve[None, :], 0.0), axis=1
    )
    set_map = (netting[:, None] == jnp.arange(NETS, dtype=jnp.int32)[None, :]).astype(jnp.float32)
    flat_pattern = pattern.reshape(-1)
    block_map = (flat_pattern[:, None] == jnp.arange(fblocks, dtype=jnp.int32)[None, :]).astype(
        jnp.float32
    )
    gathered = lax.all_gather(panels, "trade", axis=2, tiled=True)
    leading = gathered.shape[:-1]
    blocks = gathered.reshape(leading + (fblocks, block_width))
    picked = jnp.take(blocks, flat_pattern, axis=-2).reshape(
        leading + (local_blocks, PICKS, block_width)
    )
    linear = jnp.einsum(
        "...bkc,bkct->...bt", picked, lin_weight, preferred_element_type=jnp.float32
    )
    square_term = jnp.einsum(
        "...bkc,bkct->...bt", picked, quad_weight, preferred_element_type=jnp.float32
    )
    trade_state = linear + 0.25 * square_term * square_term
    block_sum = jnp.sum(positions * jax.nn.softplus(trade_state), axis=-1)
    local_exposure = norm_scale * jnp.einsum(
        "...b,bn->...n", block_sum, set_map, precision=lax.Precision.HIGHEST
    )
    local_exposure, square_term, trade_state = (local_exposure, square_term, trade_state)
    exposure = lax.psum(local_exposure, "trade")
    losses = jnp.sum(loss_given * jax.nn.softplus(exposure), axis=-1)
    charge = weights * jnp.mean(losses, axis=-1)
    exposure_grad = weights[:, None, None] * loss_given * jax.nn.sigmoid(exposure)
    block_adjoint = norm_scale * jnp.einsum(
        "...n,bn->...b", exposure_grad, set_map, precision=lax.Precision.HIGHEST
    )
    state_adjoint = block_adjoint[..., None] * positions * jax.nn.sigmoid(trade_state)
    adjoint_lin = state_adjoint.astype(jnp.bfloat16)
    adjoint_square = (0.5 * square_term * state_adjoint).astype(jnp.bfloat16)
    contrib = jnp.einsum(
        "...bt,bkct->...bkc", adjoint_lin, lin_weight, preferred_element_type=jnp.float32
    )
    contrib = contrib + jnp.einsum(
        "...bt,bkct->...bkc", adjoint_square, quad_weight, preferred_element_type=jnp.float32
    )
    leading = contrib.shape[:-3]
    flat_contrib = contrib.reshape(leading + (local_blocks * PICKS, block_width))
    leading = flat_contrib.shape[:-2]
    placed = jnp.einsum("...jc,jf->...fc", flat_contrib, block_map, precision=lax.Precision.HIGHEST)
    panel_grad = lax.psum_scatter(
        (grad_unit * placed).reshape(leading + (factors,)), "trade", scatter_dimension=2, tiled=True
    )
    return (charge, panel_grad)


def solution(mesh):
    in_specs = (
        P(None, "parts", "trade"),
        P(("parts", "trade"), None, None, None),
        P(("parts", "trade"), None, None, None),
        P(("parts", "trade"), None),
        P(("parts", "trade"), None),
        P(("parts", "trade")),
        P(),
        P(),
        P("parts"),
    )
    out_specs = (P("parts"), P(None, "parts", "trade"))
    return jax.shard_map(
        per_device, mesh=mesh, in_specs=in_specs, out_specs=out_specs, check_vma=False
    )
```

profile of v0, /device:TPU:0, one launch (start us, length us, event | category | flops | bytes accessed | tf_op | source)
XLA Modules:
  0.0 318.5 jit_solution(2586966721944326161)
XLA Ops:
  7.2 0.0 all-gather.2.cloned.1.call-start
  7.2 1.7 copy.64
  8.9 0.0 all-gather.2.cloned.1.call-update
  8.9 0.0 all-reduce.2.cloned.1.call-start
  8.9 0.8 copy.65
  9.7 0.7 compare_and_fusion
  10.4 0.1 copy.63
  10.5 0.1 reshape.88
  10.6 0.9 fusion.45
  11.5 43.4 %all-gather.2.cloned.1.call-done = bf16[2,128,4096]{1,2,0:T(8,128)(2,1)} async-done(((bf16[2,128,256]{1,2,0:T(8,128)(2,1)}), bf16[2,128,4096]{1,2,0:T(8,128)(2,1)}) %all-gather.2.cloned.1.call-update) | async-done | bytes 2097168 | tf_op jit(solution)/shard_map/all_gather | solution.py:37
  54.9 3.1 copy.66
  58.1 6.5 %gather_fusion = bf16[128,2,128,128]{3,2,1,0:T(8,128)(2,1)} fusion(bf16[2,128,32,128]{3,1,2,0:T(8,128)(2,1)S(1)} %copy.66, s32[1024]{0:T(1024)S(1)} %pad_clamp_fusion), kind=kCustom, calls=%fused_computation | custom fusion | bytes 16777728 | tf_op jit(solution)/shard_map/jit(_take)/gather | solution.py:40
  64.6 0.0 copy-start
  64.6 10.5 %copy.67 = bf16[2,128,128,128]{3,1,2,0:T(8,128)(2,1)} copy(bf16[2,128,128,128]{3,1,0,2:T(8,128)(2,1)} %bitcast.74) | data formatting | bytes 16777216 | tf_op jit(solution)/shard_map/jit(_take)/gather | solution.py:40
  75.1 0.0 copy-done
  75.1 0.0 copy-start.2
  75.1 8.4 %fusion.2 = f32[32,2,128,128,1]{2,3,4,1,0:T(8,128)} fusion(bf16[32,4,128,128]{3,2,1,0:T(8,128)(2,1)S(1)} %copy-done, bf16[2,128,32,4,128]{4,1,3,2,0:T(8,128)(2,1)} %bitcast.75, pred[32,4]{1,0:T(8,128)(4,1)S(1)} %copy.63), kind=kOutput, calls=%fused_computation.6 | convolution fusion | flops 1077936128 | bytes 16777344 | tf_op jit(solution)/shard_map/...bkc,bkct->...bt/dot_general | solution.py:46
  83.5 0.0 copy-done.2
  83.5 0.0 copy-start.4
  83.5 0.0 copy-start.3
  83.5 10.1 %fusion.8 = (f32[2,128,32]{1,0,2:T(2,128)S(1)}, f32[2,128,32,128]{1,3,0,2:T(8,128)}) fusion(f32[32,128]{1,0:T(8,128)S(1)} %copy-done.2, f32[32,2,128,128,1]{2,3,4,1,0:T(8,128)} %fusion.2, bf16[32,4,128,128]{3,2,1,0:T(8,128)(2,1)} %param.10, bf16[2,128,32,4,128]{4,1,3,2,0:T(8,128)(2,1)} %bitcast.76, pred[32,4]{1,0:T(8,128)(4,1)S(1)} %copy.63), kind=kOutput, calls=%fused_computation.13 | convolution fusion | flops 1089462272 | bytes 21020800 | tf_op jit(solution)/shard_map/...bkc,bkct->...bt/dot_general | solution.py:43
  93.6 0.0 copy-done.4
  93.6 1.0 convolution_multiply_fusion
  94.6 0.0 all-reduce.2.cloned.1.call-update
  94.6 0.2 reduce-scatter.2.cloned.1.call-start
  94.8 0.0 copy-done.3
  94.8 0.1 broadcast_multiply_fusion
  94.9 0.1 reshape.89
  95.0 85.4 %all-reduce.2.cloned.1.call-done = f32[2,128,128]{2,1,0:T(8,128)} async-done(((f32[2,128,128]{2,1,0:T(8,128)}), f32[2,128,128]{2,1,0:T(8,128)}) %all-reduce.2.cloned.1.call-update) | async-done | bytes 131088 | tf_op jit(solution)/shard_map/psum | solution.py:55
  180.5 1.1 convolution_multiply_fusion.1
  181.6 12.6 %fusion.11 = f32[32,2,128,4,128]{4,2,3,1,0:T(8,128)} fusion(bf16[32,4,128,128]{3,2,1,0:T(8,128)(2,1)} %param.10, f32[2,128,32,128]{1,3,0,2:T(8,128)} %get-tuple-element.3, f32[2,128,32]{1,0,2:T(2,128)S(1)} %copy.74, f32[32,128]{1,0:T(8,128)S(1)} %copy-done.2), kind=kOutput, calls=%fused_computation.16 | convolution fusion | flops 1080033280 | bytes 25214976 | tf_op jit(solution)/shard_map/...bt,bkct->...bkc/dot_general | solution.py:65
  194.3 17.6 %add_bitcast_fusion = f32[2,128,32,4,128]{4,1,3,0,2:T(8,128)} fusion(f32[32,2,128,4,128]{4,2,3,1,0:T(8,128)} %fusion.11, bf16[32,4,128,128]{3,2,1,0:T(8,128)(2,1)} %param.11, f32[32,2,128,128,1]{2,3,4,1,0:T(8,128)} %fusion.2, f32[2,128,32,128]{1,3,0,2:T(8,128)} %get-tuple-element.3, f32[2,128,32]{1,0,2:T(2,128)S(1)} %copy.74, f32[32,128]{1,0:T(8,128)S(1)} %copy-done.2), kind=kOutput, calls=%fused_computation.3 | convolution fusion | flops 1086324736 | bytes 46186496 | tf_op jit(solution)/shard_map/...bt,bkct->...bkc/dot_general | solution.py:68
  211.9 7.0 %copy.77 = f32[2,128,32,4,128]{4,1,3,2,0:T(8,128)S(1)} copy(f32[2,128,32,4,128]{4,1,3,0,2:T(8,128)} %add_bitcast_fusion) | data formatting | bytes 33554432 | tf_op jit(solution)/shard_map/add | solution.py:68
  218.9 14.0 %multiply_bitcast_fusion = f32[2,128,32,128]{3,2,1,0:T(8,128)} fusion(f32[2,128,128,128]{3,1,2,0:T(8,128)S(1)} %bitcast.73, s32[128]{0:T(128)S(1)} %reshape.89), kind=kOutput, calls=%fused_computation.22 | convolution fusion | flops 1611665408 | bytes 20972032 | tf_op jit(solution)/shard_map/...jc,jf->...fc/dot_general | solution.py:74
  232.9 4.9 %reshape.91 = f32[2,128,4096]{2,1,0:T(8,128)} reshape(f32[2,128,32,128]{3,2,1,0:T(8,128)} %multiply_bitcast_fusion) | data formatting | bytes 8388608 | tf_op jit(solution)/shard_map/reshape | solution.py:76
  237.8 0.0 copy-start.1
  237.8 0.0 reduce-scatter.2.cloned.1.call-update
  237.8 0.9 copy-done.1
  238.7 0.2 fusion.28
  238.9 0.5 multiply_multiply_fusion.1
  239.4 72.5 %reduce-scatter.2.cloned.1.call-done = f32[2,128,256]{2,1,0:T(8,128)} async-done(((f32[2,128,4096]{2,1,0:T(8,128)}), f32[2,128,256]{2,1,0:T(8,128)}) %reduce-scatter.2.cloned.1.call-update) | async-done | bytes 262160 | tf_op jit(solution)/shard_map/reduce_scatter | solution.py:75
  (3 shorter events, 0.0 us)
Async XLA Ops:
  7.2 47.8 %all-gather.2.cloned.1.call-start = ((), (), s32[]{:S(2)}) async-start(), calls=%async_computation.1 | async-start | bytes 2228224 | tf_op jit(solution)/shard_map/all_gather | solution.py:37
  8.9 171.6 %all-reduce.2.cloned.1.call-start = ((), (), s32[]{:S(2)}) async-start(), calls=%async_computation.2 | async-start | bytes 262144 | tf_op jit(solution)/shard_map/psum | solution.py:55
  64.6 10.5 %copy-start = (bf16[32,4,128,128]{3,2,1,0:T(8,128)(2,1)S(1)}, bf16[32,4,128,128]{3,2,1,0:T(8,128)(2,1)}, u32[]{:S(2)}) copy-start(bf16[32,4,128,128]{3,2,1,0:T(8,128)(2,1)} %param.11) | copy-start | bytes 12582916
  75.1 8.4 %copy-start.2 = (f32[32,128]{1,0:T(8,128)S(1)}, f32[32,128]{1,0:T(8,128)}, u32[]{:S(2)}) copy-start(f32[32,128]{1,0:T(8,128)} %param.12) | copy-start | bytes 49156
  83.5 10.1 %copy-start.4 = (s32[32]{0:T(128)S(1)}, s32[32]{0:T(128)}, u32[]{:S(2)}) copy-start(s32[32]{0:T(128)} %param.14) | copy-start | bytes 388
  83.5 11.3 %copy-start.3 = (f32[128]{0:T(128)S(1)}, f32[128]{0:T(128)}, u32[]{:S(2)}) copy-start(f32[128]{0:T(128)} %param.17) | copy-start | bytes 1540
  94.6 217.3 %reduce-scatter.2.cloned.1.call-start = ((), (), s32[]{:S(2)}) async-start(), calls=%async_computation.3 | async-start | bytes 4456448 | tf_op jit(solution)/shard_map/reduce_scatter | solution.py:75
  237.8 0.9 copy-start.1
Sparse Core Ops, SparseCore 0:
  10.8 44.1 all-gather.1
  94.7 85.6 all-reduce.1
  237.9 73.9 reduce-scatter.1
where the time goes:
time: 319 us; the launch traced here: 318 us
  waiting for transfers between devices  201 us (63%)
  matrix products  64.8 us (20%)
  local copies, waits for them, and re-layouts  35.8 us (11%)
  between operations  13.8 us (4%)
    psum x1, waiting for transfers between devices, per_device(): exposure = lax.psum(local_exposure, 'trade')  85.4 us
    reduce_scatter x1, waiting for transfers between devices, per_device(): lax.psum_scatter((grad_unit * placed).reshape(leading + (factors,)), 'tra...  72.5 us
    all_gather x1, waiting for transfers between devices, per_device(): gathered = lax.all_gather(panels, 'trade', axis=2, tiled=True)  43.4 us
    dot_general x1, matrix products, per_device(): jnp.einsum('...bt,bkct->...bkc', adjoint_square, quad_weight, preferred_e...  17.6 us
    gather x2, local copies, waits for them, and re-layouts, per_device(): jnp.take(blocks, flat_pattern, axis=-2)  17 us
    dot_general x1, matrix products, per_device(): jnp.einsum('...jc,jf->...fc', flat_contrib, block_map, precision=lax.Prec...  14 us
    dot_general x1, matrix products, per_device(): jnp.einsum('...bt,bkct->...bkc', adjoint_lin, lin_weight, preferred_eleme...  12.6 us
    dot_general x1, matrix products, per_device(): jnp.einsum('...bkc,bkct->...bt', picked, lin_weight, preferred_element_ty...  10.1 us
  transfers between devices with their start and end apart: 3, of which 3 were waited for; matrix products, arithmetic and copies ran while one was open for 1% of the time, Pallas kernels for 0%

commit v1 on v0

--- a/solution.py
+++ b/solution.py
@@ -1,6 +1,10 @@
+import functools
+
 import jax
 import jax.numpy as jnp
 from jax import lax
+from jax.experimental import pallas as pl
+from jax.experimental.pallas import tpu as pltpu
 from jax.sharding import PartitionSpec as P
 
 PICKS = 4
@@ -78,6 +82,464 @@
     return (charge, panel_grad)
 
 
+MESH = pl.DeviceIdType.MESH
+LANES = 128
+CORES = 2
+ROWS = 2
+TRANSPOSED = (((1,), (1,)), ((), ()))
+
+
+def fused_kernel(
+    size,
+    line,
+    norm_scale,
+    order_ref,
+    last_ref,
+    pattern_ref,
+    netting_ref,
+    dates_ref,
+    curve_ref,
+    keep_ref,
+    used_ref,
+    panels_ref,
+    positions_ref,
+    loss_ref,
+    lin_hbm,
+    quad_hbm,
+    charge_ref,
+    grad_ref,
+    lin,
+    quad,
+    panels_a,
+    panels_b,
+    slope,
+    half_square,
+    exposure_part,
+    exposure_pieces,
+    exposure_full,
+    contrib,
+    running,
+    core_out,
+    core_in,
+    kept,
+    row_out,
+    row_in,
+    line_out,
+    line_in,
+    weight_sem,
+    gather_send,
+    gather_recv,
+    piece_send,
+    piece_recv,
+    full_send,
+    full_recv,
+    core_send,
+    core_recv,
+    row_send,
+    row_recv,
+    line_send,
+    line_recv,
+):
+    me = lax.axis_index("trade")
+    core = lax.rem(me, CORES)
+    row = lax.rem(me // CORES, ROWS)
+    place = me // (CORES * ROWS)
+    blocks = positions_ref.shape[0]
+    scen = panels_ref.shape[1]
+    own = panels_ref.shape[2] // LANES
+    piece = scen // size
+    gathered = (panels_a, panels_b)
+    dates = len(gathered)
+
+    def index(z, y, c):
+        return (z * ROWS + y) * CORES + c
+
+    def along(i):
+        return lax.rem(place + i, line)
+
+    def copy(src, dst, send, recv, peer):
+        return pltpu.make_async_remote_copy(
+            src_ref=src, dst_ref=dst, send_sem=send, recv_sem=recv,
+            device_id={"trade": peer}, device_id_type=MESH,
+        )
+
+    row_peer = index(place, 1 - row, core)
+    core_peer = index(place, row, 1 - core)
+
+    weight_copies = [
+        pltpu.make_async_copy(lin_hbm, lin, weight_sem.at[0]),
+        pltpu.make_async_copy(quad_hbm, quad, weight_sem.at[1]),
+    ]
+    for each in weight_copies:
+        each.start()
+
+    for d in range(dates):
+        for h in range(own):
+            gathered[d][me * own + h] = panels_ref[d, :, h * LANES : (h + 1) * LANES]
+
+    barrier = pltpu.get_barrier_semaphore()
+
+    @pl.loop(1, size)
+    def _(i):
+        pl.semaphore_signal(
+            barrier, inc=1, device_id={"trade": lax.rem(me + i, size)}, device_id_type=MESH
+        )
+
+    pl.semaphore_wait(barrier, size - 1)
+
+    def panel_copy(d, slot, peer, k):
+        part = gathered[d].at[pl.ds(slot * own, own)]
+        return copy(part, part, gather_send.at[d, k], gather_recv.at[d, slot], peer)
+
+    def forward_to_row(d, i):
+        panel_copy(d, index(along(i), row, core), row_peer, line + i).start()
+
+    def forward_to_core(d, i, y, k):
+        panel_copy(d, index(along(i), y, core), core_peer, k).start()
+
+    def panel_wait(d, slot):
+        panel_copy(d, slot, core_peer, 0).wait_recv()
+
+    def line_step(d, i):
+        panel_wait(d, index(along(i), row, core))
+        forward_to_row(d, i)
+        forward_to_core(d, i, row, 2 * line + i)
+
+    def row_step(d, i):
+        panel_wait(d, index(along(i), 1 - row, core))
+        forward_to_core(d, i, 1 - row, 3 * line + i)
+
+    def core_steps(d):
+        for i in range(line):
+            for y in range(ROWS):
+                panel_wait(d, index(along(i), y, 1 - core))
+
+    def own_sends(d):
+        forward_to_row(d, 0)
+        forward_to_core(d, 0, row, 2 * line)
+
+    def line_sends(d):
+        for i in range(1, line):
+            panel_copy(d, me, index(along(i), row, core), i).start()
+
+    line_sends(0)
+    own_sends(0)
+    line_sends(1)
+    for i in range(1, line):
+        line_step(0, i)
+    own_sends(1)
+    for i in range(line):
+        row_step(0, i)
+    core_steps(0)
+    for each in weight_copies:
+        each.wait()
+
+    lane = lax.broadcasted_iota(jnp.int32, (1, LANES), 1)
+
+    def forward(d, first, stop):
+        @pl.loop(first, stop)
+        def _(b):
+            picked = jnp.concatenate(
+                [gathered[d][pattern_ref[b * PICKS + k]] for k in range(PICKS)], axis=1
+            )
+            both = jnp.concatenate([lin[b], quad[b]], axis=1)
+            terms = jnp.dot(picked, both, preferred_element_type=jnp.float32)
+            square = terms[:, LANES:]
+            state = terms[:, :LANES] + 0.25 * square * square
+            small = jnp.exp(-jnp.abs(state))
+            above = 1.0 + small
+            soft = jnp.maximum(state, 0.0) + jnp.log(above)
+            sigmoid = jnp.where(state >= 0.0, 1.0, small) / above
+            held = positions_ref[pl.ds(b, 1), :]
+            block_sum = jnp.sum(held * soft, axis=1, keepdims=True)
+            in_set = jnp.where(lane == netting_ref[b], norm_scale, 0.0)
+            exposure_part[d] += block_sum * in_set
+            slope[d, b] = held * sigmoid
+            half_square[d, b] = 0.5 * square
+
+    def piece_rows(t):
+        return pl.ds(pl.multiple_of(t * piece, piece), piece)
+
+    def piece_copy(d, t, source):
+        return copy(
+            exposure_part.at[d, piece_rows(t)], exposure_pieces.at[d, source],
+            piece_send.at[d, t], piece_recv.at[d, source], t,
+        )
+
+    def full_copy(d, t, source):
+        return copy(
+            exposure_full.at[d, piece_rows(source)], exposure_full.at[d, piece_rows(source)],
+            full_send.at[d, t], full_recv.at[d, source], t,
+        )
+
+    def others(act):
+        @pl.loop(1, size)
+        def _(i):
+            act(lax.rem(me + i, size))
+
+    def exposure_send(d):
+        exposure_pieces[d, me] = exposure_part[d, piece_rows(me), :]
+        others(lambda t: piece_copy(d, t, me).start())
+
+    def exposure_sum(d):
+        others(lambda t: piece_copy(d, t, t).wait_recv())
+        exposure_full[d, piece_rows(me), :] = jnp.sum(exposure_pieces[d], axis=0)
+        others(lambda t: full_copy(d, t, me).start())
+
+    def exposure_grad(d):
+        others(lambda t: full_copy(d, t, t).wait_recv())
+        exposure = exposure_full[d]
+        small = jnp.exp(-jnp.abs(exposure))
+        above = 1.0 + small
+        loss = loss_ref[...]
+        weight = curve_ref[dates_ref[d]]
+        soft = jnp.maximum(exposure, 0.0) + jnp.log(above)
+        charge_ref[d] = weight * (jnp.sum(loss * soft) * (1.0 / scen))
+        return weight * loss * (jnp.where(exposure >= 0.0, 1.0, small) / above)
+
+    def backward(d, grad, first, stop):
+        @pl.loop(first, stop)
+        def _(b):
+            in_set = jnp.where(lane == netting_ref[b], norm_scale, 0.0)
+            adjoint = jnp.sum(grad * in_set, axis=1, keepdims=True) * slope[d, b]
+            sent = jnp.concatenate(
+                [
+                    adjoint.astype(jnp.bfloat16),
+                    (half_square[d, b] * adjoint).astype(jnp.bfloat16),
+                ],
+                axis=1,
+            )
+            both = jnp.concatenate([lin[b], quad[b]], axis=1)
+            out = lax.dot_general(sent, both, TRANSPOSED, preferred_element_type=jnp.float32)
+            for k in range(PICKS):
+                contrib[b * PICKS + k] = out[:, k * LANES : (k + 1) * LANES]
+
+    def add_up():
+        running[0] = contrib[order_ref[0]]
+
+        @pl.loop(1, blocks * PICKS)
+        def _(j):
+            running[j] = contrib[order_ref[j]] + keep_ref[j] * running[j - 1]
+
+    def total(slot, h):
+        p = slot * own + h
+        return running[last_ref[p]] * used_ref[p]
+
+    def core_copy(d, y, z):
+        at = d, y * line + z
+        return copy(core_out.at[at], core_in.at[at], core_send.at[at], core_recv.at[at], core_peer)
+
+    def row_copy(d, z):
+        at = d, z
+        return copy(row_out.at[at], row_in.at[at], row_send.at[at], row_recv.at[at], row_peer)
+
+    def line_copy(d, i, here, there):
+        return copy(
+            line_out.at[d, i], line_in.at[d, here], line_send.at[d, i], line_recv.at[d, here],
+            index(there, row, core),
+        )
+
+    def core_stage(d):
+        for y in (1 - row, row):
+            @pl.loop(0, line)
+            def _(z):
+                for h in range(own):
+                    core_out[d, y * line + z, h] = total(index(z, y, 1 - core), h).astype(
+                        jnp.bfloat16
+                    )
+                core_copy(d, y, z).start()
+
+        for y in (1 - row, row):
+            @pl.loop(0, line)
+            def _(z):
+                for h in range(own):
+                    kept[d, y * line + z, h] = total(index(z, y, core), h)
+
+    def row_stage(d):
+        @pl.loop(0, line)
+        def _(z):
+            core_copy(d, 1 - row, z).wait_recv()
+            at = (1 - row) * line + z
+            row_out[d, z] = (kept[d, at] + core_in[d, at].astype(jnp.float32)).astype(jnp.bfloat16)
+            row_copy(d, z).start()
+
+    def chip_sum(d, z):
+        core_copy(d, row, z).wait_recv()
+        row_copy(d, z).wait_recv()
+        at = row * line + z
+        return (
+            kept[d, at]
+            + core_in[d, at].astype(jnp.float32)
+            + row_in[d, z].astype(jnp.float32)
+        )
+
+    def line_stage(d):
+        for i in range(1, line):
+            there = along(i)
+            line_out[d, i] = chip_sum(d, there).astype(jnp.bfloat16)
+            line_copy(d, i, place, there).start()
+
+    def finish(d):
+        found = chip_sum(d, place)
+        for i in range(1, line):
+            there = along(i)
+            line_copy(d, i, there, there).wait_recv()
+            found = found + line_in[d, there].astype(jnp.float32)
+        for h in range(own):
+            grad_ref[d, :, h * LANES : (h + 1) * LANES] = found[h] * (1.0 / norm_scale)
+
+    exposure_part[...] = jnp.zeros_like(exposure_part)
+    quarter = blocks // 4
+    for i in range(1, line):
+        forward(0, (i - 1) * quarter, i * quarter)
+        line_step(1, i)
+    forward(0, (line - 1) * quarter, blocks)
+    exposure_send(0)
+    for i in range(line):
+        row_step(1, i)
+    core_steps(1)
+    forward(1, 0, blocks // 2)
+    exposure_sum(0)
+    forward(1, blocks // 2, blocks)
+    exposure_send(1)
+    grad = exposure_grad(0)
+    backward(0, grad, 0, blocks // 2)
+    exposure_sum(1)
+    backward(0, grad, blocks // 2, blocks)
+    add_up()
+    core_stage(0)
+    grad = exposure_grad(1)
+    backward(1, grad, 0, blocks // 2)
+    row_stage(0)
+    backward(1, grad, blocks // 2, blocks)
+    add_up()
+    core_stage(1)
+    line_stage(0)
+    row_stage(1)
+    line_stage(1)
+    for d in range(dates):
+        finish(d)
+
+    for d in range(dates):
+        for k in range(1, 4 * line):
+            panel_copy(d, me, core_peer, k).wait_send()
+        others(lambda t: piece_copy(d, t, me).wait_send())
+        others(lambda t: full_copy(d, t, me).wait_send())
+        for z in range(line):
+            for y in range(ROWS):
+                core_copy(d, y, z).wait_send()
+            row_copy(d, z).wait_send()
+        for i in range(1, line):
+            line_copy(d, i, place, along(i)).wait_send()
+
+
+def per_device_fused(
+    panels,
+    lin_weight,
+    quad_weight,
+    positions,
+    pattern,
+    netting,
+    default_curve,
+    date_ids,
+    loss_given,
+):
+    size = lax.axis_size("trade")
+    line = size // (CORES * ROWS)
+    blocks, width = positions.shape
+    dates, scen, columns = panels.shape
+    own = columns // width
+    fblocks = own * size
+    terms = blocks * PICKS
+    norm_scale = (NETS / (blocks * width * size)) ** 0.5
+    flat = pattern.reshape(-1)
+    at = jnp.arange(terms, dtype=jnp.int32)
+    ahead = (flat[None, :] < flat[:, None]) | (
+        (flat[None, :] == flat[:, None]) & (at[None, :] < at[:, None])
+    )
+    rank = jnp.sum(ahead, axis=1, dtype=jnp.int32)
+    order = jnp.sum(jnp.where(rank[None, :] == at[:, None], at[None, :], 0), axis=1)
+    ids = jnp.arange(fblocks, dtype=jnp.int32)
+    first = jnp.sum(flat[None, :] < ids[:, None], axis=1, dtype=jnp.int32)
+    count = jnp.sum(flat[None, :] == ids[:, None], axis=1, dtype=jnp.int32)
+    last = jnp.maximum(first + count - 1, 0)
+    used = (count > 0).astype(jnp.float32)
+    keep = 1.0 - jnp.any(first[None, :] == at[:, None], axis=1).astype(jnp.float32)
+
+    smem = pl.BlockSpec(memory_space=pltpu.SMEM)
+    vmem = pl.BlockSpec(memory_space=pltpu.VMEM)
+    hbm = pl.BlockSpec(memory_space=pl.ANY)
+    tile = (scen, width)
+    f32, bf16 = jnp.float32, jnp.bfloat16
+    dma = pltpu.SemaphoreType.DMA
+    charge, panel_grad = pl.pallas_call(
+        functools.partial(fused_kernel, size, line, norm_scale),
+        out_shape=(
+            jax.ShapeDtypeStruct((dates,), f32),
+            jax.ShapeDtypeStruct((dates, scen, columns), f32),
+        ),
+        in_specs=[smem] * 8 + [vmem] * 3 + [hbm] * 2,
+        out_specs=(smem, vmem),
+        scratch_shapes=[
+            pltpu.VMEM((blocks, PICKS * width, width), bf16),
+            pltpu.VMEM((blocks, PICKS * width, width), bf16),
+            pltpu.VMEM((fblocks,) + tile, bf16),
+            pltpu.VMEM((fblocks,) + tile, bf16),
+            pltpu.VMEM((dates, blocks) + tile, f32),
+            pltpu.VMEM((dates, blocks) + tile, f32),
+            pltpu.VMEM((dates, scen, NETS), f32),
+            pltpu.VMEM((dates, size, scen // size, NETS), f32),
+            pltpu.VMEM((dates, scen, NETS), f32),
+            pltpu.VMEM((terms,) + tile, f32),
+            pltpu.VMEM((terms,) + tile, f32),
+            pltpu.VMEM((dates, ROWS * line, own) + tile, bf16),
+            pltpu.VMEM((dates, ROWS * line, own) + tile, bf16),
+            pltpu.VMEM((dates, ROWS * line, own) + tile, f32),
+            pltpu.VMEM((dates, line, own) + tile, bf16),
+            pltpu.VMEM((dates, line, own) + tile, bf16),
+            pltpu.VMEM((dates, line, own) + tile, bf16),
+            pltpu.VMEM((dates, line, own) + tile, bf16),
+            dma((2,)),
+            dma((dates, 4 * line)),
+            dma((dates, size)),
+            dma((dates, size)),
+            dma((dates, size)),
+            dma((dates, size)),
+            dma((dates, size)),
+            dma((dates, ROWS * line)),
+            dma((dates, ROWS * line)),
+            dma((dates, line)),
+            dma((dates, line)),
+            dma((dates, line)),
+            dma((dates, line)),
+        ],
+        compiler_params=pltpu.CompilerParams(
+            collective_id=0, has_side_effects=True, vmem_limit_bytes=56 * 1024 * 1024
+        ),
+        name="fused",
+    )(
+        order, last, flat, netting, date_ids, default_curve, keep, used,
+        panels, positions, loss_given.reshape(1, -1),
+        lin_weight.reshape(blocks, PICKS * width, width),
+        quad_weight.reshape(blocks, PICKS * width, width),
+    )
+    return (charge, panel_grad)
+
+
+def fits_kernel(mesh, panels, positions, loss_given):
+    size = mesh.shape["trade"]
+    width = positions.shape[1]
+    line = size // (CORES * ROWS)
+    return (
+        panels.shape[0] == 2
+        and width == LANES
+        and line * CORES * ROWS == size
+        and line == 4
+        and (panels.shape[2] // size) % width == 0
+        and (panels.shape[1] // mesh.shape["parts"]) % (8 * size) == 0
+    )
+
+
 def solution(mesh):
     in_specs = (
         P(None, "parts", "trade"),
@@ -91,6 +553,11 @@
         P("parts"),
     )
     out_specs = (P("parts"), P(None, "parts", "trade"))
-    return jax.shard_map(
-        per_device, mesh=mesh, in_specs=in_specs, out_specs=out_specs, check_vma=False
-    )
+
+    def run(*args):
+        body = per_device_fused if fits_kernel(mesh, args[0], args[3], args[8]) else per_device
+        return jax.shard_map(
+            body, mesh=mesh, in_specs=in_specs, out_specs=out_specs, check_vma=False
+        )(*args)
+
+    return run

time: 319 us -> 89.1 us (0.28)
  waiting for transfers between devices: 201 us -> 0 us
  Pallas kernels: 0 us -> 81.9 us
  matrix products: 64.8 us -> 0 us
  local copies, waits for them, and re-layouts: 35.8 us -> 3.73 us
  between operations: 13.8 us -> 0.66 us
    psum x1 -> x0, waiting for transfers between devices: 85.4 us -> none  [per_device(): exposure = lax.psum(local_exposure, 'trade')]
    pallas_call x0 -> x1, Pallas kernels: none -> 81.9 us  [per_device_fused(): pl.pallas_call(functools.partial(fused_kernel, size, line, norm_scale), o...]
    reduce_scatter x1 -> x0, waiting for transfers between devices: 72.5 us -> none  [per_device(): lax.psum_scatter((grad_unit * placed).reshape(leading + (factors,)), 'tra...]
    dot_general x7 -> x0, matrix products: 64.8 us -> none  [the longest x1 17.6 us: per_device(): jnp.einsum('...bt,bkct->...bkc', adjoint_square, quad_weight, preferred_e...]
    all_gather x1 -> x0, waiting for transfers between devices: 43.4 us -> none  [per_device(): gathered = lax.all_gather(panels, 'trade', axis=2, tiled=True)]
    gather x2 -> x0, local copies, waits for them, and re-layouts: 17 us -> none  [per_device(): jnp.take(blocks, flat_pattern, axis=-2)]
    reshape x4 -> x0, local copies, waits for them, and re-layouts: 8.28 us -> none  [the longest x1 4.94 us: per_device(): (grad_unit * placed).reshape(leading + (factors,))]
    add x1 -> x0, local copies, waits for them, and re-layouts: 6.99 us -> none  [per_device(): contrib + jnp.einsum('...bt,bkct->...bkc', adjoint_square, quad_weight, p...]
  transfers between devices with their start and end apart: 3 -> 0, of which waited for: 3 -> 0; matrix products, arithmetic and copies ran while one was open for 1% -> 0% of each run, Pallas kernels for 0% -> 0%
where the time goes in v1:
time: 89.1 us; the launch traced here: 88.9 us
  Pallas kernels  81.9 us (92%)
  local copies, waits for them, and re-layouts  3.73 us (4%)
  other arithmetic  2.55 us (3%)
    pallas_call x1, Pallas kernels, per_device_fused(): pl.pallas_call(functools.partial(fused_kernel, size, line, norm_scale), o...  81.9 us
    unnamed x5, local copies, waits for them, and re-layouts  3.62 us

profile of v1, /device:TPU:0, one launch (start us, length us, event | category | flops | bytes accessed | tf_op | source)
XLA Modules:
  0.0 88.9 jit_solution(6172481669273944293)
XLA Ops:
  0.6 0.8 copy.13
  1.4 0.1 lt.47.pattern_ref
  1.5 0.0 copy-start
  1.5 0.2 convert_reduce_fusion
  1.7 0.6 select_reduce_fusion.order_ref
  2.3 0.1 convert_reduce_fusion.1
  2.4 0.5 compare_convert_fusion.used_ref
  2.9 0.5 add_maximum_fusion.last_ref
  3.4 0.1 fusion.2
  3.5 0.5 convert_subtract_fusion.keep_ref
  4.1 0.0 copy-done
  4.1 81.9 %fused.1 = (f32[2]{0:T(128)}, f32[2,128,256]{2,1,0:T(8,128)}) custom-call(s32[128]{0:T(128)} %select_reduce_fusion.order_ref, s32[32]{0:T(128)} %add_maximum_fusion.last_ref, s32[128]{0:T(128)} %copy-done, s32[32]{0:T(128)} %netting_ref.1, s32[2]{0:T(128)} %dates_ref.1, f32[100]{0:T(128)} %curve_ref.1, f32[128]{0:T(128)} %convert_subtract_fusion.keep_ref, ...), custom_call_target="tpu_custom_call" | custom-call | tf_op jit(solution)/shard_map/fused/pallas_call | solution.py:475
  86.0 1.2 %copy.16 = f32[2]{0:T(128)} copy(f32[2]{0:T(128)} %get-tuple-element.6) | data formatting | bytes 16
  87.2 1.7 %copy.17 = f32[2,128,256]{2,1,0:T(8,128)} copy(f32[2,128,256]{2,1,0:T(8,128)} %get-tuple-element.7) | data formatting | bytes 524288
Async XLA Ops:
  1.5 2.6 %copy-start = (s32[128]{0:T(128)}, s32[128]{0:T(128)S(1)}, u32[]{:S(2)}) copy-start(s32[128]{0:T(128)S(1)} %lt.47.pattern_ref) | copy-start | bytes 1540

commit v2 on v1

--- a/solution.py
+++ b/solution.py
@@ -86,6 +86,7 @@
 LANES = 128
 CORES = 2
 ROWS = 2
+UNROLL = 8
 TRANSPOSED = (((1,), (1,)), ((), ()))
 
 
@@ -191,45 +192,76 @@
         part = gathered[d].at[pl.ds(slot * own, own)]
         return copy(part, part, gather_send.at[d, k], gather_recv.at[d, slot], peer)
 
-    def forward_to_row(d, i):
-        panel_copy(d, index(along(i), row, core), row_peer, line + i).start()
-
-    def forward_to_core(d, i, y, k):
-        panel_copy(d, index(along(i), y, core), core_peer, k).start()
+    def to_right(d, z):
+        return panel_copy(d, index(z, row, core), index(place + 1, row, core), z)
+
+    def to_left(d, z):
+        return panel_copy(d, index(z, row, core), index(place - 1, row, core), line + z)
+
+    def to_row(d, z):
+        return panel_copy(d, index(z, row, core), row_peer, 2 * line + z)
+
+    def to_core(d, z, y, k):
+        return panel_copy(d, index(z, y, core), core_peer, k + z)
 
     def panel_wait(d, slot):
         panel_copy(d, slot, core_peer, 0).wait_recv()
 
-    def line_step(d, i):
-        panel_wait(d, index(along(i), row, core))
-        forward_to_row(d, i)
-        forward_to_core(d, i, row, 2 * line + i)
-
-    def row_step(d, i):
-        panel_wait(d, index(along(i), 1 - row, core))
-        forward_to_core(d, i, 1 - row, 3 * line + i)
+    def goes_right(z):
+        return jnp.logical_and(z <= place, place < line - 1)
+
+    def goes_left(z):
+        return jnp.logical_and(z >= place, place > 0)
+
+    def pass_on(d, z):
+        @pl.when(goes_right(z))
+        def _():
+            to_right(d, z).start()
+
+        @pl.when(goes_left(z))
+        def _():
+            to_left(d, z).start()
+
+        to_row(d, z).start()
+        to_core(d, z, row, 3 * line).start()
+
+    def both_sides(s, act):
+        @pl.when(place >= s)
+        def _():
+            act(place - s)
+
+        if s > 0:
+            @pl.when(place + s < line)
+            def _():
+                act(place + s)
+
+    def line_step(d, s):
+        def act(z):
+            panel_wait(d, index(z, row, core))
+            pass_on(d, z)
+
+        both_sides(s, act)
+
+    def row_step(d, s):
+        def act(z):
+            panel_wait(d, index(z, 1 - row, core))
+            to_core(d, z, 1 - row, 4 * line).start()
+
+        both_sides(s, act)
 
     def core_steps(d):
-        for i in range(line):
+        for z in range(line):
             for y in range(ROWS):
-                panel_wait(d, index(along(i), y, 1 - core))
-
-    def own_sends(d):
-        forward_to_row(d, 0)
-        forward_to_core(d, 0, row, 2 * line)
-
-    def line_sends(d):
-        for i in range(1, line):
-            panel_copy(d, me, index(along(i), row, core), i).start()
-
-    line_sends(0)
-    own_sends(0)
-    line_sends(1)
-    for i in range(1, line):
-        line_step(0, i)
-    own_sends(1)
-    for i in range(line):
-        row_step(0, i)
+                panel_wait(d, index(z, y, 1 - core))
+
+    pass_on(0, place)
+    line_step(0, 1)
+    pass_on(1, place)
+    row_step(0, 0)
+    for s in range(2, line):
+        line_step(0, s)
+        row_step(0, s - 1)
+    row_step(0, line - 1)
     core_steps(0)
     for each in weight_copies:
         each.wait()
@@ -237,7 +269,7 @@
     lane = lax.broadcasted_iota(jnp.int32, (1, LANES), 1)
 
     def forward(d, first, stop):
-        @pl.loop(first, stop)
+        @pl.loop(first, stop, unroll=UNROLL)
         def _(b):
             picked = jnp.concatenate(
                 [gathered[d][pattern_ref[b * PICKS + k]] for k in range(PICKS)], axis=1
@@ -298,7 +330,7 @@
         return weight * loss * (jnp.where(exposure >= 0.0, 1.0, small) / above)
 
     def backward(d, grad, first, stop):
-        @pl.loop(first, stop)
+        @pl.loop(first, stop, unroll=UNROLL)
         def _(b):
             in_set = jnp.where(lane == netting_ref[b], norm_scale, 0.0)
             adjoint = jnp.sum(grad * in_set, axis=1, keepdims=True) * slope[d, b]
@@ -317,7 +349,7 @@
     def add_up():
         running[0] = contrib[order_ref[0]]
 
-        @pl.loop(1, blocks * PICKS)
+        @pl.loop(1, blocks * PICKS, unroll=UNROLL)
         def _(j):
             running[j] = contrib[order_ref[j]] + keep_ref[j] * running[j - 1]
 
@@ -389,18 +421,17 @@
             grad_ref[d, :, h * LANES : (h + 1) * LANES] = found[h] * (1.0 / norm_scale)
 
     exposure_part[...] = jnp.zeros_like(exposure_part)
-    quarter = blocks // 4
-    for i in range(1, line):
-        forward(0, (i - 1) * quarter, i * quarter)
-        line_step(1, i)
-    forward(0, (line - 1) * quarter, blocks)
+    share = blocks // line
+    for s in range(1, line):
+        forward(0, (s - 1) * share, s * share)
+        line_step(1, s)
+        row_step(1, s - 1)
+    forward(0, (line - 1) * share, blocks)
     exposure_send(0)
-    for i in range(line):
-        row_step(1, i)
+    row_step(1, line - 1)
     core_steps(1)
-    forward(1, 0, blocks // 2)
     exposure_sum(0)
-    forward(1, blocks // 2, blocks)
+    forward(1, 0, blocks)
     exposure_send(1)
     grad = exposure_grad(0)
     backward(0, grad, 0, blocks // 2)
@@ -414,15 +445,25 @@
     backward(1, grad, blocks // 2, blocks)
     add_up()
     core_stage(1)
-    line_stage(0)
     row_stage(1)
-    line_stage(1)
+    for d in range(dates):
+        line_stage(d)
     for d in range(dates):
         finish(d)
 
     for d in range(dates):
-        for k in range(1, 4 * line):
-            panel_copy(d, me, core_peer, k).wait_send()
+        for z in range(line):
+            @pl.when(goes_right(z))
+            def _():
+                to_right(d, z).wait_send()
+
+            @pl.when(goes_left(z))
+            def _():
+                to_left(d, z).wait_send()
+
+            to_row(d, z).wait_send()
+            to_core(d, z, row, 3 * line).wait_send()
+            to_core(d, z, 1 - row, 4 * line).wait_send()
         others(lambda t: piece_copy(d, t, me).wait_send())
         others(lambda t: full_copy(d, t, me).wait_send())
         for z in range(line):
@@ -500,7 +541,7 @@
             pltpu.VMEM((dates, line, own) + tile, bf16),
             pltpu.VMEM((dates, line, own) + tile, bf16),
             dma((2,)),
-            dma((dates, 4 * line)),
+            dma((dates, 5 * line)),
             dma((dates, size)),
             dma((dates, size)),
             dma((dates, size)),

time: 89.1 us -> 72.9 us (0.82)
  Pallas kernels: 81.9 us -> 65.8 us
    pallas_call x1, Pallas kernels: 81.9 us -> 65.8 us  [per_device_fused(): pl.pallas_call(functools.partial(fused_kernel, size, line, norm_scale), o...]
where the time goes in v2:
time: 72.9 us; the launch traced here: 72.7 us
  Pallas kernels  65.8 us (90%)
  local copies, waits for them, and re-layouts  3.73 us (5%)
  other arithmetic  2.55 us (3%)
    pallas_call x1, Pallas kernels, per_device_fused(): pl.pallas_call(functools.partial(fused_kernel, size, line, norm_scale), o...  65.8 us
    unnamed x5, local copies, waits for them, and re-layouts  3.62 us

profile of v2, /device:TPU:0, one launch (start us, length us, event | category | flops | bytes accessed | tf_op | source)
XLA Modules:
  0.0 72.7 jit_solution(14062731338794275791)
XLA Ops:
  0.6 0.8 %copy.13 = s32[32,4]{1,0:T(8,128)S(1)} copy(s32[32,4]{0,1:T(4,128)} %param.13) | data formatting | bytes 1024 | tf_op args[4]
  1.4 0.1 lt.47.pattern_ref
  1.5 0.0 copy-start
  1.5 0.2 convert_reduce_fusion
  1.7 0.6 select_reduce_fusion.order_ref
  2.3 0.1 convert_reduce_fusion.1
  2.4 0.5 compare_convert_fusion.used_ref
  2.9 0.5 add_maximum_fusion.last_ref
  3.4 0.1 fusion.2
  3.5 0.5 convert_subtract_fusion.keep_ref
  4.1 0.0 copy-done
  4.1 65.8 %fused.1 = (f32[2]{0:T(128)}, f32[2,128,256]{2,1,0:T(8,128)}) custom-call(s32[128]{0:T(128)} %select_reduce_fusion.order_ref, s32[32]{0:T(128)} %add_maximum_fusion.last_ref, s32[128]{0:T(128)} %copy-done, s32[32]{0:T(128)} %netting_ref.1, s32[2]{0:T(128)} %dates_ref.1, f32[100]{0:T(128)} %curve_ref.1, f32[128]{0:T(128)} %convert_subtract_fusion.keep_ref, ...), custom_call_target="tpu_custom_call" | custom-call | tf_op jit(solution)/shard_map/fused/pallas_call | solution.py:516
  69.9 1.2 %copy.16 = f32[2]{0:T(128)} copy(f32[2]{0:T(128)} %get-tuple-element.6) | data formatting | bytes 16
  71.1 1.7 %copy.17 = f32[2,128,256]{2,1,0:T(8,128)} copy(f32[2,128,256]{2,1,0:T(8,128)} %get-tuple-element.7) | data formatting | bytes 524288
Async XLA Ops:
  1.5 2.6 %copy-start = (s32[128]{0:T(128)}, s32[128]{0:T(128)S(1)}, u32[]{:S(2)}) copy-start(s32[128]{0:T(128)S(1)} %lt.47.pattern_ref) | copy-start | bytes 1540

commit v3 on v2

--- a/solution.py
+++ b/solution.py
@@ -94,14 +94,11 @@
     size,
     line,
     norm_scale,
-    order_ref,
-    last_ref,
+    plan_ref,
     pattern_ref,
     netting_ref,
     dates_ref,
     curve_ref,
-    keep_ref,
-    used_ref,
     panels_ref,
     positions_ref,
     loss_ref,
@@ -149,6 +146,8 @@
     scen = panels_ref.shape[1]
     own = panels_ref.shape[2] // LANES
     piece = scen // size
+    terms = blocks * PICKS
+    fblocks = own * size
     gathered = (panels_a, panels_b)
     dates = len(gathered)
 
@@ -255,12 +254,15 @@
                 panel_wait(d, index(z, y, 1 - core))
 
     pass_on(0, place)
+    pass_on(1, place)
     line_step(0, 1)
-    pass_on(1, place)
     row_step(0, 0)
     for s in range(2, line):
+        line_step(1, s - 1)
         line_step(0, s)
+        row_step(1, s - 2)
         row_step(0, s - 1)
+    line_step(1, line - 1)
     row_step(0, line - 1)
     core_steps(0)
     for each in weight_copies:
@@ -347,15 +349,17 @@
                 contrib[b * PICKS + k] = out[:, k * LANES : (k + 1) * LANES]
 
     def add_up():
-        running[0] = contrib[order_ref[0]]
-
-        @pl.loop(1, blocks * PICKS, unroll=UNROLL)
+        running[0] = contrib[plan_ref[0]]
+
+        @pl.loop(1, terms, unroll=UNROLL)
         def _(j):
-            running[j] = contrib[order_ref[j]] + keep_ref[j] * running[j - 1]
+            keep = plan_ref[terms + j].astype(jnp.float32)
+            running[j] = contrib[plan_ref[j]] + keep * running[j - 1]
 
     def total(slot, h):
         p = slot * own + h
-        return running[last_ref[p]] * used_ref[p]
+        used = plan_ref[2 * terms + fblocks + p].astype(jnp.float32)
+        return running[plan_ref[2 * terms + p]] * used
 
     def core_copy(d, y, z):
         at = d, y * line + z
@@ -373,8 +377,9 @@
 
     def core_stage(d):
         for y in (1 - row, row):
-            @pl.loop(0, line)
-            def _(z):
+            @pl.loop(1, line + 1)
+            def _(i):
+                z = along(i)
                 for h in range(own):
                     core_out[d, y * line + z, h] = total(index(z, y, 1 - core), h).astype(
                         jnp.bfloat16
@@ -387,13 +392,12 @@
                 for h in range(own):
                     kept[d, y * line + z, h] = total(index(z, y, core), h)
 
-    def row_stage(d):
-        @pl.loop(0, line)
-        def _(z):
-            core_copy(d, 1 - row, z).wait_recv()
-            at = (1 - row) * line + z
-            row_out[d, z] = (kept[d, at] + core_in[d, at].astype(jnp.float32)).astype(jnp.bfloat16)
-            row_copy(d, z).start()
+    def row_part(d, i):
+        z = along(i)
+        core_copy(d, 1 - row, z).wait_recv()
+        at = (1 - row) * line + z
+        row_out[d, z] = (kept[d, at] + core_in[d, at].astype(jnp.float32)).astype(jnp.bfloat16)
+        row_copy(d, z).start()
 
     def chip_sum(d, z):
         core_copy(d, row, z).wait_recv()
@@ -405,11 +409,10 @@
             + row_in[d, z].astype(jnp.float32)
         )
 
-    def line_stage(d):
-        for i in range(1, line):
-            there = along(i)
-            line_out[d, i] = chip_sum(d, there).astype(jnp.bfloat16)
-            line_copy(d, i, place, there).start()
+    def line_part(d, i):
+        there = along(i)
+        line_out[d, i] = chip_sum(d, there).astype(jnp.bfloat16)
+        line_copy(d, i, place, there).start()
 
     def finish(d):
         found = chip_sum(d, place)
@@ -422,32 +425,36 @@
 
     exposure_part[...] = jnp.zeros_like(exposure_part)
     share = blocks // line
-    for s in range(1, line):
-        forward(0, (s - 1) * share, s * share)
-        line_step(1, s)
-        row_step(1, s - 1)
-    forward(0, (line - 1) * share, blocks)
+    forward(0, 0, share)
+    for s in range(line - 2, line):
+        row_step(1, s)
+        forward(0, (s - line + 3) * share, (s - line + 4) * share)
+    forward(0, 3 * share, blocks)
     exposure_send(0)
-    row_step(1, line - 1)
     core_steps(1)
+    forward(1, 0, 2 * share)
     exposure_sum(0)
-    forward(1, 0, blocks)
+    forward(1, 2 * share, blocks)
     exposure_send(1)
     grad = exposure_grad(0)
-    backward(0, grad, 0, blocks // 2)
+    backward(0, grad, 0, 2 * share)
     exposure_sum(1)
-    backward(0, grad, blocks // 2, blocks)
+    backward(0, grad, 2 * share, blocks)
     add_up()
     core_stage(0)
     grad = exposure_grad(1)
-    backward(1, grad, 0, blocks // 2)
-    row_stage(0)
-    backward(1, grad, blocks // 2, blocks)
+    backward(1, grad, 0, share)
+    for i in range(1, line + 1):
+        row_part(0, i)
+    backward(1, grad, share, blocks)
     add_up()
     core_stage(1)
-    row_stage(1)
-    for d in range(dates):
-        line_stage(d)
+    for i in range(1, line):
+        line_part(0, i)
+        row_part(1, i)
+    row_part(1, line)
+    for i in range(1, line):
+        line_part(1, i)
     for d in range(dates):
         finish(d)
 
@@ -504,8 +511,9 @@
     first = jnp.sum(flat[None, :] < ids[:, None], axis=1, dtype=jnp.int32)
     count = jnp.sum(flat[None, :] == ids[:, None], axis=1, dtype=jnp.int32)
     last = jnp.maximum(first + count - 1, 0)
-    used = (count > 0).astype(jnp.float32)
-    keep = 1.0 - jnp.any(first[None, :] == at[:, None], axis=1).astype(jnp.float32)
+    used = jnp.minimum(count, 1)
+    keep = 1 - jnp.max((first[None, :] == at[:, None]).astype(jnp.int32), axis=1)
+    plan = jnp.concatenate([order, keep, last, used])
 
     smem = pl.BlockSpec(memory_space=pltpu.SMEM)
     vmem = pl.BlockSpec(memory_space=pltpu.VMEM)
@@ -519,7 +527,7 @@
             jax.ShapeDtypeStruct((dates,), f32),
             jax.ShapeDtypeStruct((dates, scen, columns), f32),
         ),
-        in_specs=[smem] * 8 + [vmem] * 3 + [hbm] * 2,
+        in_specs=[smem] * 5 + [vmem] * 3 + [hbm] * 2,
         out_specs=(smem, vmem),
         scratch_shapes=[
             pltpu.VMEM((blocks, PICKS * width, width), bf16),
@@ -559,7 +567,7 @@
         ),
         name="fused",
     )(
-        order, last, flat, netting, date_ids, default_curve, keep, used,
+        plan, flat, netting, date_ids, default_curve,
         panels, positions, loss_given.reshape(1, -1),
         lin_weight.reshape(blocks, PICKS * width, width),
         quad_weight.reshape(blocks, PICKS * width, width),

time: 72.9 us -> 66.2 us (0.908)
  Pallas kernels: 65.8 us -> 60.4 us
  other arithmetic: 2.55 us -> 1.16 us
    pallas_call x1, Pallas kernels: 65.8 us -> 60.4 us  [per_device_fused(): pl.pallas_call(functools.partial(fused_kernel, size, line, norm_scale), o...]
where the time goes in v3:
time: 66.2 us; the launch traced here: 66 us
  Pallas kernels  60.4 us (91%)
  local copies, waits for them, and re-layouts  3.72 us (6%)
  other arithmetic  1.16 us (2%)
  between operations  0.68 us (1%)
    pallas_call x1, Pallas kernels, per_device_fused(): pl.pallas_call(functools.partial(fused_kernel, size, line, norm_scale), o...  60.4 us
    unnamed x5, local copies, waits for them, and re-layouts  3.61 us

profile of v3, /device:TPU:0, one launch (start us, length us, event | category | flops | bytes accessed | tf_op | source)
XLA Modules:
  0.0 66.0 jit_solution(17203563370960430858)
XLA Ops:
  0.6 0.8 %copy.13 = s32[32,4]{1,0:T(8,128)S(1)} copy(s32[32,4]{0,1:T(4,128)} %param.13) | data formatting | bytes 1024 | tf_op args[4]
  1.4 0.1 lt.47.pattern_ref
  1.5 0.0 copy-start
  1.5 0.2 convert_reduce_fusion
  1.7 0.1 select_reduce_fusion
  1.8 0.1 convert_reduce_fusion.3
  1.9 0.1 convert_reduce_fusion.2
  2.0 0.7 pad_add_fusion.plan_ref
  2.7 0.0 copy-done
  2.7 60.4 %fused.1 = (f32[2]{0:T(128)}, f32[2,128,256]{2,1,0:T(8,128)}) custom-call(s32[320]{0:T(512)} %pad_add_fusion.plan_ref, s32[128]{0:T(128)} %copy-done, s32[32]{0:T(128)} %netting_ref.1, s32[2]{0:T(128)} %dates_ref.1, f32[100]{0:T(128)} %curve_ref.1, bf16[2,128,256]{2,1,0:T(8,128)(2,1)} %panels_ref.1, f32[32,128]{1,0:T(8,128)} %positions_ref.1, ...), custom_call_target="tpu_custom_call" | custom-call | tf_op jit(solution)/shard_map/fused/pallas_call | solution.py:524
  63.2 1.2 %copy.16 = f32[2]{0:T(128)} copy(f32[2]{0:T(128)} %get-tuple-element.8) | data formatting | bytes 16
  64.3 1.7 %copy.17 = f32[2,128,256]{2,1,0:T(8,128)} copy(f32[2,128,256]{2,1,0:T(8,128)} %get-tuple-element.9) | data formatting | bytes 524288
  (2 shorter events, 0.0 us)
Async XLA Ops:
  1.5 1.2 %copy-start = (s32[128]{0:T(128)}, s32[128]{0:T(128)S(1)}, u32[]{:S(2)}) copy-start(s32[128]{0:T(128)S(1)} %lt.47.pattern_ref) | copy-start | bytes 1540

commit v4 on v3

--- a/solution.py
+++ b/solution.py
@@ -307,7 +307,7 @@
         )
 
     def others(act):
-        @pl.loop(1, size)
+        @pl.loop(1, size, unroll=5)
         def _(i):
             act(lax.rem(me + i, size))
 
@@ -377,7 +377,7 @@
 
     def core_stage(d):
         for y in (1 - row, row):
-            @pl.loop(1, line + 1)
+            @pl.loop(1, line + 1, unroll=line)
             def _(i):
                 z = along(i)
                 for h in range(own):
@@ -387,7 +387,7 @@
                 core_copy(d, y, z).start()
 
         for y in (1 - row, row):
-            @pl.loop(0, line)
+            @pl.loop(0, line, unroll=line)
             def _(z):
                 for h in range(own):
                     kept[d, y * line + z, h] = total(index(z, y, core), h)

time: 66.2 us -> 65.8 us (level)
  no operation moved by 1% of the time
where the time goes in v4:
time: 65.8 us; the launch traced here: 65.6 us
  Pallas kernels  60 us (91%)
  local copies, waits for them, and re-layouts  3.72 us (6%)
  other arithmetic  1.16 us (2%)
  between operations  0.68 us (1%)
    pallas_call x1, Pallas kernels, per_device_fused(): pl.pallas_call(functools.partial(fused_kernel, size, line, norm_scale), o...  60 us
    unnamed x5, local copies, waits for them, and re-layouts  3.61 us

profile of v4, /device:TPU:0, one launch (start us, length us, event | category | flops | bytes accessed | tf_op | source)
XLA Modules:
  0.0 65.6 jit_solution(6199913046253604750)
XLA Ops:
  0.6 0.8 %copy.13 = s32[32,4]{1,0:T(8,128)S(1)} copy(s32[32,4]{0,1:T(4,128)} %param.13) | data formatting | bytes 1024 | tf_op args[4]
  1.4 0.1 lt.47.pattern_ref
  1.5 0.0 copy-start
  1.5 0.2 convert_reduce_fusion
  1.7 0.1 select_reduce_fusion
  1.8 0.1 convert_reduce_fusion.3
  1.9 0.1 convert_reduce_fusion.2
  2.0 0.7 pad_add_fusion.plan_ref
  2.7 0.0 copy-done
  2.7 60.0 %fused.1 = (f32[2]{0:T(128)}, f32[2,128,256]{2,1,0:T(8,128)}) custom-call(s32[320]{0:T(512)} %pad_add_fusion.plan_ref, s32[128]{0:T(128)} %copy-done, s32[32]{0:T(128)} %netting_ref.1, s32[2]{0:T(128)} %dates_ref.1, f32[100]{0:T(128)} %curve_ref.1, bf16[2,128,256]{2,1,0:T(8,128)(2,1)} %panels_ref.1, f32[32,128]{1,0:T(8,128)} %positions_ref.1, ...), custom_call_target="tpu_custom_call" | custom-call | tf_op jit(solution)/shard_map/fused/pallas_call | solution.py:524
  62.7 1.2 %copy.16 = f32[2]{0:T(128)} copy(f32[2]{0:T(128)} %get-tuple-element.8) | data formatting | bytes 16
  63.9 1.7 %copy.17 = f32[2,128,256]{2,1,0:T(8,128)} copy(f32[2,128,256]{2,1,0:T(8,128)} %get-tuple-element.9) | data formatting | bytes 524288
  (2 shorter events, 0.0 us)
Async XLA Ops:
  1.5 1.2 %copy-start = (s32[128]{0:T(128)}, s32[128]{0:T(128)S(1)}, u32[]{:S(2)}) copy-start(s32[128]{0:T(128)S(1)} %lt.47.pattern_ref) | copy-start | bytes 1540
